TPU v7x, 256 devices: a whole 4x4x8 slice. The times are simulated.
256 devices in a mesh: rows: 32 (over y_lo, z, core), pairs: 8 (over x, y_hi).
Axes of the slice: x: 4, y: 4 (y_hi: 2, y_lo: 2; y = y_hi * 2 + y_lo), z: 8, core: 2. Of those that a mesh axis runs over, the one named last changes fastest.
Arguments:
- slab_active: float32 [64, 64, 4096], P('rows', None, 'pairs'), may hold values from -6 to 6
- slab_general: float32 [64, 1536, 4096], P('rows', None, 'pairs'), may hold values from -6 to 6
- kappa_general: float32 [1536, 64], P('rows'), may hold values from -0.15625 to 0.15625
- kappa_window: float32 [64, 64], P('rows'), as said below
- density_one: float32 [4096], P('pairs'), may hold values from -0.09375 to 0.09375
- density_two: bfloat16 [64, 64, 4096], P(None, None, 'pairs'), may hold values from -0.01171875 to 0.01171875
Outputs:
- sigma_vector: float32 [64, 64], P('rows')
Inputs may be any that keep to these rules, and one draw needn't show every extreme that they name: kappa_window is antisymmetric: kappa_window[p, q] = -kappa_window[q, p] exactly, with zero diagonal.
All inputs are finite; a program needn't handle non-finite values.
Results may differ from a plain program's by a relative error of at most 0.0003.
Values sent between devices are 32-bit elements; how exact they have to be, the bound alone decides.
A program may use at most 64 MiB of HBM per device.

v0:
```python
import jax
import jax.numpy as jnp
from jax import lax
from jax.sharding import PartitionSpec as P


def per_device(slab_active, slab_general, kappa_general, kappa_window, density_one, density_two):
    highest = lax.Precision.HIGHEST
    density_wide = density_two.astype(jnp.float32)
    moved = jnp.einsum(
        "pqc,qt->ptc",
        slab_general,
        lax.all_gather(kappa_general, "rows", axis=0, tiled=True),
        precision=highest,
    )
    coulomb_part = jnp.einsum("ptc,c->pt", moved, density_one, precision=highest)
    turned = jnp.einsum(
        "pq,qtc->ptc",
        kappa_window,
        lax.all_gather(slab_active, "rows", axis=0, tiled=True),
        precision=highest,
    )
    total = moved + turned
    exchange_part = jnp.einsum("puc,tuc->pt", total, density_wide, precision=highest)
    reduced = lax.psum((exchange_part, coulomb_part), "pairs")
    return 2.0 * (reduced[0] + 2.0 * reduced[1])


def solution(mesh):
    in_specs = (
        P("rows", None, "pairs"),
        P("rows", None, "pairs"),
        P("rows", None),
        P("rows", None),
        P("pairs"),
        P(None, None, "pairs"),
    )
    out_specs = P("rows", None)
    return jax.shard_map(
        per_device, mesh=mesh, in_specs=in_specs, out_specs=out_specs, check_vma=False
    )
```

profile of v0, /device:TPU:1, one launch (start us, length us, event | category | flops | bytes accessed | tf_op | source)
XLA Modules:
  0.0 138.9 jit_solution(16201201574582430114)
XLA Ops:
  6.5 0.0 copy-start
  6.5 0.0 all-gather.2.cloned.1.call-start
  6.5 0.7 all-gather.2.cloned.1.call-update
  7.3 41.3 %all_gather.6 = f32[1536,64]{1,0:T(8,128)S(1)} all-gather(f32[48,64]{1,0:T(8,128)} %param.8), channel_id=1, replica_groups=mesh['rows'=32,'pairs'=8] {'rows'}, dimensions={0}, use_global_device_ids=true | all-gather | bytes 405504 | tf_op jit(solution)/shard_map/all_gather | solution.py:13
  48.6 38.5 %all-gather.2.cloned.1.call-done = f32[64,64,512]{2,1,0:T(8,128)} async-done(((f32[2,64,512]{2,1,0:T(8,128)}), f32[64,64,512]{2,1,0:T(8,128)}) %all-gather.2.cloned.1.call-update) | async-done | bytes 8388624 | tf_op jit(solution)/shard_map/all_gather | solution.py:20
  87.1 0.0 copy-start.1
  87.1 0.0 copy-start.2
  87.1 12.6 %fusion = f32[2,64,512]{2,0,1:T(2,128)S(1)} fusion(f32[64,64,512]{2,1,0:T(8,128)} %all-gather.2.cloned.1.call-done, f32[2,64]{1,0:T(2,128)} %param.9), kind=kOutput, calls=%fused_computation | convolution fusion | flops 50331648 | bytes 8651264 | tf_op jit(solution)/shard_map/pq,qtc->ptc/dot_general | solution.py:17
  99.7 0.0 copy-done.1
  99.7 4.0 %copy_add_fusion = (f32[2,64,512]{2,1,0:T(8,128)S(1)}, f32[2,64,512]{2,1,0:T(8,128)S(1)}) fusion(f32[2,64,512]{2,0,1:T(2,128)S(1)} %fusion, f32[2,1536,512]{2,1,0:T(8,128)S(1)} %copy-done.1, f32[1536,64]{1,0:T(8,128)S(1)} %all_gather.6), kind=kOutput, calls=%fused_computation.7 | convolution fusion | flops 1208025088 | bytes 7471104 | tf_op jit(solution)/shard_map/pqc,qt->ptc/dot_general | solution.py:10
  103.7 0.0 copy-done.2
  103.7 8.4 %fusion.4 = f32[2,64]{1,0:T(2,128)S(1)} fusion(bf16[64,64,512]{2,1,0:T(8,128)(2,1)S(1)} %copy-done.2, f32[2,64,512]{2,1,0:T(8,128)S(1)} %get-tuple-element.7), kind=kOutput, calls=%fused_computation.5 | convolution fusion | flops 50331648 | bytes 4456960 | tf_op jit(solution)/shard_map/puc,tuc->pt/dot_general | solution.py:24
  112.2 0.0 copy-done
  112.2 0.4 fusion.10
  112.6 18.9 %all-reduce = (f32[2,64]{1,0:T(2,128)S(1)}, f32[2,64]{1,0:T(2,128)S(1)}) all-reduce(f32[2,64]{1,0:T(2,128)S(1)} %fusion.4, f32[2,64]{1,0:T(2,128)S(1)} %bitcast.19), channel_id=1, replica_groups=mesh['rows'=32,'pairs'=8] {'pairs'}, use_global_device_ids=true, to_apply=%region_0.0 | all-reduce | flops 256 | bytes 2048 | tf_op jit(solution)/shard_map/psum | solution.py:25
  131.5 0.6 add_multiply_fusion
Async XLA Ops:
  6.5 105.6 %copy-start = (f32[512]{0:T(512)S(1)}, f32[512]{0:T(512)}, u32[]{:S(2)}) copy-start(f32[512]{0:T(512)} %param.10) | copy-start | bytes 6148
  6.5 80.5 %all-gather.2.cloned.1.call-start = ((), (), s32[]{:S(2)}) async-start(), calls=%async_computation | async-start | bytes 8650752 | tf_op jit(solution)/shard_map/all_gather | solution.py:20
  87.1 12.6 %copy-start.1 = (f32[2,1536,512]{2,1,0:T(8,128)S(1)}, f32[2,1536,512]{2,1,0:T(8,128)}, u32[]{:S(2)}) copy-start(f32[2,1536,512]{2,1,0:T(8,128)} %param.7) | copy-start | bytes 18874372
  87.1 16.7 %copy-start.2 = (bf16[64,64,512]{2,1,0:T(8,128)(2,1)S(1)}, bf16[64,64,512]{2,1,0:T(8,128)(2,1)}, u32[]{:S(2)}) copy-start(bf16[64,64,512]{2,1,0:T(8,128)(2,1)} %param.11) | copy-start | bytes 12582916
Sparse Core Ops, SparseCore 0:
  9.2 77.7 all-gather.1
where the time goes:
time: 142 us; the launch traced here: 139 us
  blocking collectives  60.2 us (42%)
  waiting for transfers between devices  39.2 us (28%)
  matrix products  25.5 us (18%)
  between operations  13.4 us (9%)
    all_gather x1, blocking collectives, per_device(): lax.all_gather(kappa_general, 'rows', axis=0, tiled=True)  41.3 us
    all_gather x1, waiting for transfers between devices, per_device(): lax.all_gather(slab_active, 'rows', axis=0, tiled=True)  38.5 us
    psum x1, blocking collectives, per_device(): reduced = lax.psum((exchange_part, coulomb_part), 'pairs')  18.9 us
    dot_general x1, matrix products, per_device(): jnp.einsum('pq,qtc->ptc', kappa_window, lax.all_gather(slab_active, 'rows...  12.6 us
    dot_general x1, matrix products, per_device(): jnp.einsum('puc,tuc->pt', total, density_wide, precision=highest)  8.43 us
    dot_general x1, matrix products, per_device(): jnp.einsum('pqc,qt->ptc', slab_general, lax.all_gather(kappa_general, 'ro...  4.05 us
  transfers between devices with their start and end apart: 1, of which 1 were waited for; matrix products, arithmetic and copies ran while one was open for 0% of the time, Pallas kernels for 0%

commit v1 on v0

v1 whole, which is shorter than its diff:
```python
import jax
import jax.numpy as jnp
from jax import lax
from jax.experimental import pallas as pl
from jax.experimental.pallas import tpu as pltpu
from jax.sharding import PartitionSpec as P

MESH = pl.DeviceIdType.MESH
BF16, F32 = jnp.bfloat16, jnp.float32
ROW_BY_ROW = (((1,), (1,)), ((), ()))
PLAIN = (((1,), (0,)), ((), ()))

NEAR = ((0, 0), (0, 1), (0, 7), (1, 0), (0, 2), (0, 6), (1, 1), (1, 7))
FAR = ((0, 3), (0, 5), (1, 2), (1, 6), (0, 4), (1, 3), (1, 5), (1, 4))
PLACES = (NEAR, FAR)
SEND_ORDER = tuple(reversed(FAR)) + tuple(reversed(NEAR[1:]))


def slot_of(dy, dz):
    for chunk in range(2):
        if (dy, dz) in PLACES[chunk]:
            return chunk, PLACES[chunk].index((dy, dz))


def split(x):
    high = x.astype(BF16)
    return high, (x - high.astype(F32)).astype(BF16)


def cross(d2_ref, w_ref, s8_ref):
    sub = lax.broadcasted_iota(jnp.int32, (8, 256), 0)
    lane = lax.broadcasted_iota(jnp.int32, (8, 256), 1) % 64
    masks = [lane == sub + 8 * k for k in range(8)]
    group = 8
    for b in range(64 // group):
        r = lax.dot_general(
            d2_ref[b * group:(b + 1) * group].reshape(group * 64, 512), w_ref[...], ROW_BY_ROW,
            preferred_element_type=F32,
        )
        for t in range(group):
            acc = jnp.zeros((8, 256), F32)
            for k in range(8):
                at = (t * 8 + k) * 8
                acc = jnp.where(masks[k], r[at:at + 8, :], acc)
            s8_ref[b * group + t] = acc


def as_row(s8_ref):
    s = jnp.sum(s8_ref[...], axis=1).T
    pair = jnp.sum(s.reshape(2, 2, 64, 64), axis=(0, 2))
    return jnp.concatenate([pair[0:1], pair[1:2]], axis=1)


def kernel(
    sa_hbm, g_hbm, kg_hbm, kw_hbm, d1_hbm, d2_hbm, out_ref,
    sa, gbuf, kgin, kw, d1, d2, ghi, glo, kgbuf, left, w, s8, moved, fall, pbuf,
    load_sem, kg_send, kg_recv, f_send, f_recv, sib_send, sib_recv, p_send, p_recv,
):
    row, pair = lax.axis_index("rows"), lax.axis_index("pairs")
    core = row % 2
    chip = row // 2
    ylo, z = chip // 8, chip % 8

    def chip_at(dy, dz):
        return lax.rem(ylo + dy, 2) * 8 + lax.rem(z + dz, 8)

    def peer(dy, dz):
        return (chip_at(dy, dz) * 2 + core, pair)

    sibling = (chip * 2 + 1 - core, pair)
    pair_peers = [(row, lax.rem(pair + k, 8)) for k in range(1, 8)]

    kg_load = pltpu.make_async_copy(kg_hbm, kgin, load_sem.at[0])
    kg_load.start()
    barrier = pltpu.get_barrier_semaphore()
    for dy, dz in SEND_ORDER:
        pl.semaphore_signal(barrier, inc=1, device_id=peer(dy, dz), device_id_type=MESH)
    for dev in pair_peers + [sibling]:
        pl.semaphore_signal(barrier, inc=1, device_id=dev, device_id_type=MESH)
    sa_load = pltpu.make_async_copy(sa_hbm, sa, load_sem.at[1])
    sa_load.start()
    d2_load = pltpu.make_async_copy(d2_hbm, d2, load_sem.at[2])
    d2_load.start()
    d1_load = pltpu.make_async_copy(d1_hbm, d1, load_sem.at[3])
    d1_load.start()
    kw_load = pltpu.make_async_copy(kw_hbm, kw, load_sem.at[4])
    kw_load.start()
    g_loads = []
    for p in range(2):
        for h in range(2):
            load = pltpu.make_async_copy(
                g_hbm.at[p, :, pl.ds(h * 24, 24), :], gbuf.at[p, h], load_sem.at[5 + 2 * p + h]
            )
            load.start()
            g_loads.append(load)

    kg_load.wait()
    kgbuf[0, core, 0] = jnp.concatenate([kgin[0:24, :], kgin[24:48, :]], axis=1)
    pl.semaphore_wait(barrier, 23)

    kg_copies = {}
    for n, (dy, dz) in enumerate(SEND_ORDER):
        chunk, slot = slot_of(dy, (8 - dz) % 8)
        copy = pltpu.make_async_remote_copy(
            kgbuf.at[0, core, 0], kgbuf.at[chunk, core, slot], kg_send.at[n], kg_recv.at[chunk, slot],
            device_id=peer(dy, dz), device_id_type=MESH,
        )
        copy.start()
        kg_copies[chunk, slot] = copy

    sa_load.wait()
    high, low = split(sa[...].reshape(128, 512))
    w[0:128] = high
    w[128:256] = low
    d2_load.wait()
    cross(d2, w, s8)
    fall[core, chip] = as_row(s8)
    f_copies = []
    for n, (dy, dz) in enumerate(SEND_ORDER):
        copy = pltpu.make_async_remote_copy(
            fall.at[core, chip], fall.at[core, chip], f_send.at[n], f_recv.at[n],
            device_id=peer(dy, dz), device_id_type=MESH,
        )
        copy.start()
        f_copies.append(copy)

    for load in g_loads:
        load.wait()

    def split_general(n, _):
        p, h, c = n // 4, (n // 2) % 2, n % 2
        for chunk in range(2):
            for s in range(0, 8, 2):
                first, second = (chip_at(*PLACES[chunk][s + i]) * 2 + c for i in range(2))
                both = jnp.concatenate([gbuf[p, h, first], gbuf[p, h, second]], axis=0)
                a, b = split(both)
                ghi[chunk, p, h, c, s * 24:s * 24 + 48, :] = a
                glo[chunk, p, h, c, s * 24:s * 24 + 48, :] = b
        return 0

    lax.fori_loop(0, 8, split_general, 0)

    def hand_over(chunk):
        for slot in range(8):
            if (chunk, slot) != (0, 0):
                kg_copies[chunk, slot].wait_recv()
        copy = pltpu.make_async_remote_copy(
            kgbuf.at[chunk, core], kgbuf.at[chunk, core], sib_send.at[chunk], sib_recv.at[chunk],
            device_id=sibling, device_id_type=MESH,
        )
        copy.start()
        return copy

    def rotate(chunk):
        x = kgbuf[chunk].reshape(384, 128).T
        high, low = split(jnp.concatenate([x[0:64], x[64:128]], axis=1))
        left[0:64] = high
        left[64:128] = low
        for p in range(2):
            gh = ghi[chunk, p].reshape(768, 512)
            gl = glo[chunk, p].reshape(768, 512)
            a = lax.dot_general(left[...], gh, PLAIN, preferred_element_type=F32)
            b = lax.dot_general(left[0:64], gl, PLAIN, preferred_element_type=F32)
            part = a[0:64] + a[64:128] + b
            moved[p] = part if chunk == 0 else moved[p] + part

    near = hand_over(0)
    near.wait_recv()
    rotate(0)
    far = hand_over(1)

    for copy in f_copies:
        copy.wait_recv()
    f_over = pltpu.make_async_remote_copy(
        fall.at[core], fall.at[core], sib_send.at[2], sib_recv.at[2], device_id=sibling, device_id_type=MESH,
    )
    f_over.start()

    far.wait_recv()
    rotate(1)
    high, low = split(moved[...].reshape(128, 512))
    w[0:128] = high
    w[128:256] = low
    cross(d2, w, s8)
    exchange = as_row(s8)

    d1_load.wait()
    high, low = split(jnp.broadcast_to(d1[...], (16, 512)))
    at = lax.broadcasted_iota(jnp.int32, (16, 512), 0)
    ones = jnp.where(at == 0, high.astype(F32), jnp.where(at == 1, low.astype(F32), 0.0)).astype(BF16)
    c = lax.dot_general(ones, w[...], ROW_BY_ROW, preferred_element_type=F32)
    c = c[0:1] + c[1:2]
    coulomb = c[:, 0:128] + c[:, 128:256]

    kw_load.wait()
    f_over.wait_recv()
    lane = lax.broadcasted_iota(jnp.int32, (1, 128), 1)
    acc = [jnp.zeros((1, 128), F32) for _ in range(2)]
    for k in range(16):
        for c in range(2):
            f = fall[c, k]
            for p in range(2):
                q = 4 * k + 2 * c
                acc[p] = acc[p] + f * jnp.where(lane < 64, kw[p, q], kw[p, q + 1])
    turned = jnp.concatenate([a[:, 0:64] + a[:, 64:128] for a in acc], axis=1)

    pbuf[pair] = exchange + 2.0 * coulomb + turned
    p_copies = []
    for n, dev in enumerate(pair_peers):
        copy = pltpu.make_async_remote_copy(
            pbuf.at[pair], pbuf.at[pair], p_send.at[n], p_recv.at[n], device_id=dev, device_id_type=MESH,
        )
        copy.start()
        p_copies.append(copy)
    for copy in p_copies:
        copy.wait_recv()
    total = pbuf[0]
    for k in range(1, 8):
        total = total + pbuf[k]
    total = 2.0 * total
    out_ref[0:1, :] = total[:, 0:64]
    out_ref[1:2, :] = total[:, 64:128]

    for copy in list(kg_copies.values()) + f_copies + p_copies + [near, far, f_over]:
        copy.wait_send()


def per_device(slab_active, slab_general, kappa_general, kappa_window, density_one, density_two):
    dma = pltpu.SemaphoreType.DMA
    return pl.pallas_call(
        kernel,
        out_shape=jax.ShapeDtypeStruct((2, 64), F32),
        in_specs=[pl.BlockSpec(memory_space=pl.ANY)] * 6,
        out_specs=pl.BlockSpec(memory_space=pltpu.VMEM),
        scratch_shapes=[
            pltpu.VMEM((2, 64, 512), F32),
            pltpu.VMEM((2, 2, 32, 24, 512), F32),
            pltpu.VMEM((48, 64), F32),
            pltpu.SMEM((2, 64), F32),
            pltpu.VMEM((1, 512), F32),
            pltpu.VMEM((64, 64, 512), BF16),
            pltpu.VMEM((2, 2, 2, 2, 192, 512), BF16),
            pltpu.VMEM((2, 2, 2, 2, 192, 512), BF16),
            pltpu.VMEM((2, 2, 8, 24, 128), F32),
            pltpu.VMEM((128, 768), BF16),
            pltpu.VMEM((256, 512), BF16),
            pltpu.VMEM((64, 8, 256), F32),
            pltpu.VMEM((2, 64, 512), F32),
            pltpu.VMEM((2, 16, 1, 128), F32),
            pltpu.VMEM((8, 1, 128), F32),
            dma((9,)),
            dma((15,)),
            dma((2, 8)),
            dma((15,)),
            dma((15,)),
            dma((3,)),
            dma((3,)),
            dma((7,)),
            dma((7,)),
        ],
        compiler_params=pltpu.CompilerParams(
            collective_id=0, has_side_effects=True, vmem_limit_bytes=48 * 2**20
        ),
        name="sigma",
    )(
        slab_active,
        slab_general.reshape(2, 32, 48, 512),
        kappa_general,
        kappa_window,
        density_one.reshape(1, 512),
        density_two,
    )


def solution(mesh):
    in_specs = (
        P("rows", None, "pairs"),
        P("rows", None, "pairs"),
        P("rows", None),
        P("rows", None),
        P("pairs"),
        P(None, None, "pairs"),
    )
    out_specs = P("rows", None)
    return jax.shard_map(
        per_device, mesh=mesh, in_specs=in_specs, out_specs=out_specs, check_vma=False
    )
```

time: 142 us -> 32.4 us (0.23); the launches traced: 139 us -> 32.2 us
  blocking collectives: 60.2 us -> 0 us
  waiting for transfers between devices: 39.2 us -> 0 us
  Pallas kernels: 0 us -> 26.4 us
  matrix products: 25.5 us -> 0 us
  between operations: 13.4 us -> 0.01 us
  local copies, waits for them, and re-layouts: 0.01 us -> 5.8 us
    all_gather x1 -> x0, blocking collectives: 41.3 us -> none  [per_device(): lax.all_gather(kappa_general, 'rows', axis=0, tiled=True)]
    all_gather x1 -> x0, waiting for transfers between devices: 38.5 us -> none  [per_device(): lax.all_gather(slab_active, 'rows', axis=0, tiled=True)]
    pallas_call x0 -> x1, Pallas kernels: none -> 26.4 us  [per_device(): pl.pallas_call(kernel, out_shape=jax.ShapeDtypeStruct((2, 64), F32), in_s...]
    dot_general x4 -> x0, matrix products: 25.5 us -> none  [the longest x1 12.6 us: per_device(): jnp.einsum('pq,qtc->ptc', kappa_window, lax.all_gather(slab_active, 'rows...]
    psum x1 -> x0, blocking collectives: 18.9 us -> none  [per_device(): reduced = lax.psum((exchange_part, coulomb_part), 'pairs')]
    unnamed x6 -> x11, local copies, waits for them, and re-layouts: 0.01 us -> 5.8 us
  transfers between devices with their start and end apart: 1 -> 0, of which waited for: 1 -> 0; matrix products, arithmetic and copies ran while one was open for 0% -> 0% of each run, Pallas kernels for 0% -> 0%
where the time goes in v1:
time: 32.4 us; the launch traced here: 32.2 us
  Pallas kernels  26.4 us (81%)
  local copies, waits for them, and re-layouts  5.8 us (18%)
    pallas_call x1, Pallas kernels, per_device(): pl.pallas_call(kernel, out_shape=jax.ShapeDtypeStruct((2, 64), F32), in_s...  26.4 us
    unnamed x11, local copies, waits for them, and re-layouts  5.8 us

profile of v1, /device:TPU:1, one launch (start us, length us, event | category | flops | bytes accessed | tf_op | source)
XLA Modules:
  0.0 32.2 jit_solution(16408060231809577506)
XLA Ops:
  0.0 0.0 copy-start
  0.0 2.2 %copy-done = bf16[64,64,512]{2,1,0:T(8,128)(2,1)S(1)} copy-done((bf16[64,64,512]{2,1,0:T(8,128)(2,1)S(1)}, bf16[64,64,512]{2,1,0:T(8,128)(2,1)}, u32[]{:S(2)}) %copy-start) | copy-done | bytes 4194328
  2.2 0.0 copy-start.1
  2.2 0.9 %copy-done.1 = f32[2,64,512]{2,1,0:T(8,128)S(1)} copy-done((f32[2,64,512]{2,1,0:T(8,128)S(1)}, f32[2,64,512]{2,1,0:T(8,128)}, u32[]{:S(2)}) %copy-start.1) | copy-done | bytes 262168
  3.1 0.0 copy-start.2
  3.1 0.7 %copy-done.2 = f32[48,64]{1,0:T(8,128)S(1)} copy-done((f32[48,64]{1,0:T(8,128)S(1)}, f32[48,64]{1,0:T(8,128)}, u32[]{:S(2)}) %copy-start.2) | copy-done | bytes 12312
  3.9 0.0 copy-start.3
  3.9 0.7 %copy-done.3 = f32[512]{0:T(512)S(1)} copy-done((f32[512]{0:T(512)S(1)}, f32[512]{0:T(512)}, u32[]{:S(2)}) %copy-start.3) | copy-done | bytes 2072
  4.6 0.0 copy-start.4
  4.6 0.7 %copy-done.4 = f32[2,64]{1,0:T(2,128)S(1)} copy-done((f32[2,64]{1,0:T(2,128)S(1)}, f32[2,64]{1,0:T(2,128)}, u32[]{:S(2)}) %copy-start.4) | copy-done | bytes 536
  5.2 26.4 %sigma.1 = f32[2,64]{1,0:T(2,128)S(1)} custom-call(f32[2,64,512]{2,1,0:T(8,128)S(1)} %copy-done.1, f32[2,32,48,512]{3,2,1,0:T(8,128)} %bitcast.3, f32[48,64]{1,0:T(8,128)S(1)} %copy-done.2, f32[2,64]{1,0:T(2,128)S(1)} %copy-done.4, f32[1,512]{1,0:T(1,128)S(1)} %bitcast.2, bf16[64,64,512]{2,1,0:T(8,128)(2,1)S(1)} %copy-done), custom_call_target="tpu_custom_call" | custom-call | tf_op jit(solution)/shard_map/sigma/pallas_call | solution.py:230
  31.6 0.6 %copy.8 = f32[2,64]{1,0:T(2,128)} copy(f32[2,64]{1,0:T(2,128)S(1)} %sigma.1) | data formatting | bytes 1024
Async XLA Ops:
  0.0 2.2 %copy-start = (bf16[64,64,512]{2,1,0:T(8,128)(2,1)S(1)}, bf16[64,64,512]{2,1,0:T(8,128)(2,1)}, u32[]{:S(2)}) copy-start(bf16[64,64,512]{2,1,0:T(8,128)(2,1)} %d2_hbm.1) | copy-start | bytes 12582916
  2.2 0.9 %copy-start.1 = (f32[2,64,512]{2,1,0:T(8,128)S(1)}, f32[2,64,512]{2,1,0:T(8,128)}, u32[]{:S(2)}) copy-start(f32[2,64,512]{2,1,0:T(8,128)} %sa_hbm.1) | copy-start | bytes 786436
  3.1 0.7 %copy-start.2 = (f32[48,64]{1,0:T(8,128)S(1)}, f32[48,64]{1,0:T(8,128)}, u32[]{:S(2)}) copy-start(f32[48,64]{1,0:T(8,128)} %kg_hbm.1) | copy-start | bytes 36868
  3.9 0.7 %copy-start.3 = (f32[512]{0:T(512)S(1)}, f32[512]{0:T(512)}, u32[]{:S(2)}) copy-start(f32[512]{0:T(512)} %param.10) | copy-start | bytes 6148
  4.6 0.7 %copy-start.4 = (f32[2,64]{1,0:T(2,128)S(1)}, f32[2,64]{1,0:T(2,128)}, u32[]{:S(2)}) copy-start(f32[2,64]{1,0:T(2,128)} %kw_hbm.1) | copy-start | bytes 1540

commit v2 on v1

--- a/solution.py
+++ b/solution.py
@@ -54,7 +54,7 @@
 def kernel(
     sa_hbm, g_hbm, kg_hbm, kw_hbm, d1_hbm, d2_hbm, out_ref,
     sa, gbuf, kgin, kw, d1, d2, ghi, glo, kgbuf, left, w, s8, moved, fall, pbuf,
-    load_sem, kg_send, kg_recv, f_send, f_recv, sib_send, sib_recv, p_send, p_recv,
+    load_sem, here, kg_send, kg_recv, f_send, f_recv, sib_send, sib_recv, p_send, p_recv,
 ):
     row, pair = lax.axis_index("rows"), lax.axis_index("pairs")
     core = row % 2
@@ -67,16 +67,38 @@
     def peer(dy, dz):
         return (chip_at(dy, dz) * 2 + core, pair)
 
+    def is_later(dy, dz):
+        return lax.rem(z + dz, 8) * 2 + lax.rem(ylo + dy, 2) > z * 2 + ylo
+
+    def number(dy, dz):
+        return SEND_ORDER.index((dy, dz))
+
     sibling = (chip * 2 + 1 - core, pair)
-    pair_peers = [(row, lax.rem(pair + k, 8)) for k in range(1, 8)]
+    pair_peers = [lax.rem(pair + k, 8) for k in range(1, 8)]
 
     kg_load = pltpu.make_async_copy(kg_hbm, kgin, load_sem.at[0])
     kg_load.start()
     barrier = pltpu.get_barrier_semaphore()
+    earlier = core
     for dy, dz in SEND_ORDER:
-        pl.semaphore_signal(barrier, inc=1, device_id=peer(dy, dz), device_id_type=MESH)
-    for dev in pair_peers + [sibling]:
-        pl.semaphore_signal(barrier, inc=1, device_id=dev, device_id_type=MESH)
+        later = is_later(dy, dz)
+        earlier = earlier + jnp.where(later, 0, 1)
+
+        @pl.when(later)
+        def _():
+            pl.semaphore_signal(barrier, inc=1, device_id=peer(dy, dz), device_id_type=MESH)
+
+    for other in pair_peers:
+        earlier = earlier + jnp.where(other > pair, 0, 1)
+
+        @pl.when(other > pair)
+        def _():
+            pl.semaphore_signal(barrier, inc=1, device_id=(row, other), device_id_type=MESH)
+
+    @pl.when(core == 0)
+    def _():
+        pl.semaphore_signal(barrier, inc=1, device_id=sibling, device_id_type=MESH)
+
     sa_load = pltpu.make_async_copy(sa_hbm, sa, load_sem.at[1])
     sa_load.start()
     d2_load = pltpu.make_async_copy(d2_hbm, d2, load_sem.at[2])
@@ -96,17 +118,46 @@
 
     kg_load.wait()
     kgbuf[0, core, 0] = jnp.concatenate([kgin[0:24, :], kgin[24:48, :]], axis=1)
-    pl.semaphore_wait(barrier, 23)
+
+    @pl.when(earlier > 0)
+    def _():
+        pl.semaphore_wait(barrier, earlier)
 
     kg_copies = {}
     for n, (dy, dz) in enumerate(SEND_ORDER):
         chunk, slot = slot_of(dy, (8 - dz) % 8)
-        copy = pltpu.make_async_remote_copy(
+        kg_copies[dy, dz] = pltpu.make_async_remote_copy(
             kgbuf.at[0, core, 0], kgbuf.at[chunk, core, slot], kg_send.at[n], kg_recv.at[chunk, slot],
             device_id=peer(dy, dz), device_id_type=MESH,
         )
-        copy.start()
-        kg_copies[chunk, slot] = copy
+    for dy, dz in SEND_ORDER:
+
+        @pl.when(jnp.logical_not(is_later(dy, dz)))
+        def _():
+            pl.semaphore_signal(
+                here.at[number(dy, (8 - dz) % 8)], inc=1, device_id=peer(dy, dz), device_id_type=MESH
+            )
+            kg_copies[dy, dz].start()
+
+    @pl.when(core == 1)
+    def _():
+        pl.semaphore_signal(here.at[15], inc=1, device_id=sibling, device_id_type=MESH)
+
+    for n, other in enumerate(pair_peers):
+
+        @pl.when(other < pair)
+        def _():
+            pl.semaphore_signal(here.at[16 + 6 - n], inc=1, device_id=(row, other), device_id_type=MESH)
+
+    def serve_later(places):
+        for dy, dz in places:
+
+            @pl.when(is_later(dy, dz))
+            def _():
+                pl.semaphore_wait(here.at[number(dy, dz)], 1)
+                kg_copies[dy, dz].start()
+
+    serve_later(NEAR[1:])
 
     sa_load.wait()
     high, low = split(sa[...].reshape(128, 512))
@@ -115,6 +166,7 @@
     d2_load.wait()
     cross(d2, w, s8)
     fall[core, chip] = as_row(s8)
+    serve_later(FAR)
     f_copies = []
     for n, (dy, dz) in enumerate(SEND_ORDER):
         copy = pltpu.make_async_remote_copy(
@@ -140,10 +192,14 @@
 
     lax.fori_loop(0, 8, split_general, 0)
 
+    @pl.when(core == 0)
+    def _():
+        pl.semaphore_wait(here.at[15], 1)
+
     def hand_over(chunk):
         for slot in range(8):
             if (chunk, slot) != (0, 0):
-                kg_copies[chunk, slot].wait_recv()
+                kg_copies[tuple((8 - a) % 8 if i else a for i, a in enumerate(PLACES[chunk][slot]))].wait_recv()
         copy = pltpu.make_async_remote_copy(
             kgbuf.at[chunk, core], kgbuf.at[chunk, core], sib_send.at[chunk], sib_recv.at[chunk],
             device_id=sibling, device_id_type=MESH,
@@ -206,9 +262,14 @@
 
     pbuf[pair] = exchange + 2.0 * coulomb + turned
     p_copies = []
-    for n, dev in enumerate(pair_peers):
+    for n, other in enumerate(pair_peers):
+
+        @pl.when(other > pair)
+        def _():
+            pl.semaphore_wait(here.at[16 + n], 1)
+
         copy = pltpu.make_async_remote_copy(
-            pbuf.at[pair], pbuf.at[pair], p_send.at[n], p_recv.at[n], device_id=dev, device_id_type=MESH,
+            pbuf.at[pair], pbuf.at[pair], p_send.at[n], p_recv.at[n], device_id=(row, other), device_id_type=MESH,
         )
         copy.start()
         p_copies.append(copy)
@@ -230,7 +291,7 @@
     return pl.pallas_call(
         kernel,
         out_shape=jax.ShapeDtypeStruct((2, 64), F32),
-        in_specs=[pl.BlockSpec(memory_space=pl.ANY)] * 6,
+        in_specs=[pl.BlockSpec(memory_space=pltpu.HBM)] * 6,
         out_specs=pl.BlockSpec(memory_space=pltpu.VMEM),
         scratch_shapes=[
             pltpu.VMEM((2, 64, 512), F32),
@@ -249,6 +310,7 @@
             pltpu.VMEM((2, 16, 1, 128), F32),
             pltpu.VMEM((8, 1, 128), F32),
             dma((9,)),
+            pltpu.SemaphoreType.REGULAR((23,)),
             dma((15,)),
             dma((2, 8)),
             dma((15,)),
@@ -262,14 +324,17 @@
             collective_id=0, has_side_effects=True, vmem_limit_bytes=48 * 2**20
         ),
         name="sigma",
-    )(
-        slab_active,
-        slab_general.reshape(2, 32, 48, 512),
-        kappa_general,
-        kappa_window,
-        density_one.reshape(1, 512),
-        density_two,
-    )
+    )(*(
+        pltpu.with_memory_space_constraint(x, pltpu.HBM)
+        for x in (
+            slab_active,
+            slab_general.reshape(2, 32, 48, 512),
+            kappa_general,
+            kappa_window,
+            density_one.reshape(1, 512),
+            density_two,
+        )
+    ))
 
 
 def solution(mesh):

time: 32.4 us -> 27.2 us (0.84)
  local copies, waits for them, and re-layouts: 5.8 us -> 0.56 us
    unnamed x11 -> x1, local copies, waits for them, and re-layouts: 5.8 us -> 0.56 us
where the time goes in v2:
time: 27.2 us
  Pallas kernels  26.6 us (98%)
  local copies, waits for them, and re-layouts  0.56 us (2%)
    pallas_call x1, Pallas kernels, per_device(): pl.pallas_call(kernel, out_shape=jax.ShapeDtypeStruct((2, 64), F32), in_s...  26.6 us
    unnamed x1, local copies, waits for them, and re-layouts  0.56 us

profile of v2, /device:TPU:1, one launch (start us, length us, event | category | flops | bytes accessed | tf_op | source)
XLA Modules:
  0.0 27.2 jit_solution(3600431431694773811)
XLA Ops:
  0.0 26.6 %sigma.1 = f32[2,64]{1,0:T(2,128)S(1)} custom-call(f32[2,64,512]{2,1,0:T(8,128)} %sa_hbm.1, f32[2,32,48,512]{3,2,1,0:T(8,128)} %bitcast.2, f32[48,64]{1,0:T(8,128)} %kg_hbm.1, f32[2,64]{1,0:T(2,128)} %kw_hbm.1, f32[1,512]{1,0:T(1,128)} %bitcast.3, bf16[64,64,512]{2,1,0:T(8,128)(2,1)} %d2_hbm.1), custom_call_target="tpu_custom_call" | custom-call | tf_op jit(solution)/shard_map/sigma/pallas_call | solution.py:291
  26.6 0.6 %copy.8 = f32[2,64]{1,0:T(2,128)} copy(f32[2,64]{1,0:T(2,128)S(1)} %sigma.1) | data formatting | bytes 1024

commit v3 on v1

v3 whole, which is shorter than its diff:
```python
import jax
import jax.numpy as jnp
from jax import lax
from jax.experimental import pallas as pl
from jax.experimental.pallas import tpu as pltpu
from jax.sharding import PartitionSpec as P

MESH = pl.DeviceIdType.MESH
BF16, F32 = jnp.bfloat16, jnp.float32
ROW_BY_ROW = (((1,), (1,)), ((), ()))
PLAIN = (((1,), (0,)), ((), ()))

OWN = ((1, 3), (1, 2), (0, 3), (1, 1), (0, 2), (1, 0), (0, 1))
CUT = ((1, 1), (0, 1), (1, 2), (1, 0), (0, 2), (0, 0), (1, 3), (0, 3))
DIRECT = ((1, 1), (0, 1), (1, 3), (0, 3))
ALL = tuple((1, *o) for o in CUT) + tuple((0, *o) for o in OWN)


def own_slot(dy, dk):
    return dy * 4 + dk


def cut_slot(dy, dk):
    return dk * 2 + dy


def f_slot(cut, dy, dk):
    return 8 + cut_slot(dy, dk) if cut else own_slot(dy, dk)


def split(x):
    high = x.astype(BF16)
    return high, (x - high.astype(F32)).astype(BF16)


def cross(d2_ref, w_ref, s8_ref):
    sub = lax.broadcasted_iota(jnp.int32, (8, 256), 0)
    lane = lax.broadcasted_iota(jnp.int32, (8, 256), 1) % 64
    masks = [lane == sub + 8 * k for k in range(8)]
    group = 8
    for b in range(64 // group):
        r = lax.dot_general(
            d2_ref[b * group:(b + 1) * group].reshape(group * 64, 512), w_ref[...], ROW_BY_ROW,
            preferred_element_type=F32,
        )
        for t in range(group):
            acc = jnp.zeros((8, 256), F32)
            for k in range(8):
                at = (t * 8 + k) * 8
                acc = jnp.where(masks[k], r[at:at + 8, :], acc)
            s8_ref[b * group + t] = acc


def as_row(s8_ref):
    s = jnp.sum(s8_ref[...], axis=1).T
    pair = jnp.sum(s.reshape(2, 2, 64, 64), axis=(0, 2))
    return jnp.concatenate([pair[0:1], pair[1:2]], axis=1)


def kernel(
    sa_hbm, g_hbm, kg_hbm, kw_hbm, d1_hbm, d2_hbm, out_ref,
    sa, gbuf, kgin, kw, d1, d2, ghi, glo, kg, left, w, s8, moved, fall, pbuf,
    load_sem, near_here, far_here, hop_here, own_send, own_recv, cut_send, cut_recv, pass_send, pass_recv,
    sib_send, sib_recv, f_send, f_recv, p_send, p_recv,
):
    row, pair = lax.axis_index("rows"), lax.axis_index("pairs")
    core, chip = row % 2, row // 2
    ylo, z = chip // 8, chip % 8
    half, k = z // 4, z % 4
    x, yhi = pair // 2, pair % 2
    early, late = half == 0, half == 1

    def chip_of(cut, dy, dk):
        return (ylo ^ dy) * 8 + (half ^ cut) * 4 + (k ^ dk)

    def peer(cut, dy, dk):
        return (chip_of(cut, dy, dk) * 2 + core, pair)

    def signal(semaphore, device):
        pl.semaphore_signal(semaphore, inc=1, device_id=device, device_id_type=MESH)

    def remote(source, target, send, recv, device):
        return pltpu.make_async_remote_copy(
            source, target, send, recv, device_id=device, device_id_type=MESH
        )

    def is_later(dy, dk):
        return (k ^ dk) * 2 + (ylo ^ dy) > k * 2 + ylo

    sibling = (chip * 2 + 1 - core, pair)
    beside = [((chip ^ 1) * 2 + core, pair), ((chip ^ 1) * 2 + 1 - core, pair)]
    pair_peers = [lax.rem(pair + n, 8) for n in range(1, 8)]
    y = yhi * 2 + ylo

    def at(x, y, z):
        return (((y % 2) * 8 + z) * 2 + core, x * 2 + y // 2)

    hops = (
        (at((x + 1) % 4, y, z), None),
        (at((x + 3) % 4, y, z), None),
        (at(x, (y + 1) % 4, z), None),
        (at(x, (y + 3) % 4, z), None),
        (at(x, y, (z + 1) % 8), k < 3),
        (at(x, y, (z + 7) % 8), k > 0),
        (sibling, None),
    )

    def for_hops(condition, act):
        for n, (device, there) in enumerate(hops):
            @pl.when(condition if there is None else jnp.logical_and(condition, there))
            def _():
                act(n, device)

    kg_load = pltpu.make_async_copy(kg_hbm, kgin, load_sem.at[0])
    kg_load.start()

    barrier = pltpu.get_barrier_semaphore()

    @pl.when(early)
    def _():
        for dy, dk in CUT:
            signal(barrier, peer(1, dy, dk))
        for other in pair_peers:
            signal(barrier, (row, other))
        signal(barrier, sibling)
        signal(barrier, beside[1])
        for dy, dk in OWN:
            @pl.when(is_later(dy, dk))
            def _():
                signal(barrier, peer(0, dy, dk))

    for_hops(late, lambda n, device: signal(barrier, device))

    sa_load = pltpu.make_async_copy(sa_hbm, sa, load_sem.at[1])
    sa_load.start()
    d2_load = pltpu.make_async_copy(d2_hbm, d2, load_sem.at[2])
    d2_load.start()
    d1_load = pltpu.make_async_copy(d1_hbm, d1, load_sem.at[3])
    d1_load.start()
    kw_load = pltpu.make_async_copy(kw_hbm, kw, load_sem.at[4])
    kw_load.start()
    g_loads = []
    for p in range(2):
        for h in range(2):
            load = pltpu.make_async_copy(
                g_hbm.at[p, :, pl.ds(h * 24, 24), :], gbuf.at[p, h], load_sem.at[5 + 2 * p + h]
            )
            load.start()
            g_loads.append(load)

    kg_load.wait()
    kg[0, core, 0] = jnp.concatenate([kgin[0:24, :], kgin[24:48, :]], axis=1)
    pl.semaphore_wait(barrier, jnp.where(early, 9 + 2 * k + ylo, 14 + jnp.where(jnp.logical_or(k == 0, k == 3), 0, 1)))

    own = {}
    for n, (dy, dk) in enumerate(OWN):
        own[dy, dk] = remote(
            kg.at[0, core, 0], kg.at[0, core, own_slot(dy, dk)], own_send.at[n], own_recv.at[n], peer(0, dy, dk)
        )
    cut = {}
    for n, (dy, dk) in enumerate(DIRECT):
        cut[dy, dk] = remote(
            kg.at[0, core, 0], kg.at[1, core, cut_slot(dy, dk)], cut_send.at[n], cut_recv.at[n], peer(1, dy, dk)
        )

    @pl.when(late)
    def _():
        for copy in cut.values():
            copy.start()
        for n, (dy, dk) in enumerate(CUT):
            signal(far_here.at[n], peer(1, dy, dk))
        for_hops(late, lambda n, device: signal(hop_here.at[0, n ^ 1 if n < 6 else n], device))

    @pl.when(early)
    def _():
        for n, (dy, dk) in enumerate(OWN):
            @pl.when(jnp.logical_not(is_later(dy, dk)))
            def _():
                signal(near_here.at[n], peer(0, dy, dk))
                own[dy, dk].start()

    sa_load.wait()
    high, low = split(sa[...].reshape(128, 512))
    w[0:128] = high
    w[128:256] = low
    d2_load.wait()
    cross(d2, w, s8)
    fall[core, 0] = as_row(s8)
    f_copies = {}
    for n, (c, dy, dk) in enumerate(ALL):
        f_copies[c, dy, dk] = remote(
            fall.at[core, 0], fall.at[core, f_slot(c, dy, dk)], f_send.at[n], f_recv.at[n], peer(c, dy, dk)
        )

    @pl.when(late)
    def _():
        for dy, dk in CUT:
            f_copies[1, dy, dk].start()
        for step in range(3):
            for_hops(late, lambda n, device: pl.semaphore_wait(hop_here.at[step, n], 1))
            if step < 2:
                for_hops(late, lambda n, device: signal(hop_here.at[step + 1, n ^ 1 if n < 6 else n], device))
        for dy, dk in OWN:
            own[dy, dk].start()
        for dy, dk in OWN:
            f_copies[0, dy, dk].start()

    @pl.when(early)
    def _():
        for n, (dy, dk) in enumerate(OWN):
            @pl.when(is_later(dy, dk))
            def _():
                pl.semaphore_wait(near_here.at[n], 1)
                own[dy, dk].start()
        for dy, dk in OWN:
            f_copies[0, dy, dk].start()

    for load in g_loads:
        load.wait()

    def split_general(n, _):
        p, h, c = n // 4, (n // 2) % 2, n % 2
        for part, chips in ((0, [chip_of(0, i // 4, i % 4) for i in range(8)]), (1, [chip_of(1, i % 2, i // 2) for i in range(8)])):
            for s in range(0, 8, 2):
                both = jnp.concatenate([gbuf[p, h, chips[s] * 2 + c], gbuf[p, h, chips[s + 1] * 2 + c]], axis=0)
                a, b = split(both)
                ghi[part, p, h, c, s * 24:s * 24 + 48, :] = a
                glo[part, p, h, c, s * 24:s * 24 + 48, :] = b
        return 0

    lax.fori_loop(0, 8, split_general, 0)

    @pl.when(early)
    def _():
        for n, (dy, dk) in enumerate(CUT):
            pl.semaphore_wait(far_here.at[n], 1)
            if (dy, dk) in DIRECT:
                cut[dy, dk].start()
        for dy, dk in CUT:
            f_copies[1, dy, dk].start()

    passes = {}
    for n, dk in enumerate((3, 1)):
        mine = kg.at[1, core, pl.ds(2 * dk, 2)]
        theirs = kg.at[1, core, pl.ds(2 * (dk ^ 1), 2)]
        for m, (target, device) in enumerate(((theirs, beside[0]), (theirs, beside[1]), (mine, sibling))):
            passes[n, m] = remote(mine, target, pass_send.at[n, m], pass_recv.at[n, m], device)

    def pass_on():
        for n, dk in enumerate((3, 1)):
            for dy in range(2):
                cut[dy, dk].wait_recv()
            for m in range(3):
                passes[n, m].start()

    def rotate(part):
        x = kg[part].reshape(384, 128).T
        high, low = split(jnp.concatenate([x[0:64], x[64:128]], axis=1))
        left[0:64] = high
        left[64:128] = low
        result = []
        for p in range(2):
            gh = ghi[part, p].reshape(768, 512)
            gl = glo[part, p].reshape(768, 512)
            a = lax.dot_general(left[...], gh, PLAIN, preferred_element_type=F32)
            b = lax.dot_general(left[0:64], gl, PLAIN, preferred_element_type=F32)
            result.append(a[0:64] + a[64:128] + b)
        return result

    pass_on()
    for copy in own.values():
        copy.wait_recv()
    over = remote(kg.at[0, core], kg.at[0, core], sib_send.at[0], sib_recv.at[0], sibling)
    over.start()
    over.wait_recv()
    for p, part in enumerate(rotate(0)):
        moved[p] = part

    for copy in f_copies.values():
        copy.wait_recv()
    f_over = remote(fall.at[core], fall.at[core], sib_send.at[1], sib_recv.at[1], sibling)
    f_over.start()
    d1_load.wait()
    high, low = split(jnp.broadcast_to(d1[...], (16, 512)))
    line = lax.broadcasted_iota(jnp.int32, (16, 512), 0)
    ones = jnp.where(line == 0, high.astype(F32), jnp.where(line == 1, low.astype(F32), 0.0)).astype(BF16)
    kw_load.wait()
    f_over.wait_recv()
    lane = lax.broadcasted_iota(jnp.int32, (1, 128), 1)
    acc = [jnp.zeros((1, 128), F32) for _ in range(2)]
    for c, dy, dk in ((0, 0, 0),) + ALL:
        first = 4 * chip_of(c, dy, dk)
        for n in range(2):
            f = fall[n, f_slot(c, dy, dk)]
            for p in range(2):
                q = first + 2 * n
                acc[p] = acc[p] + f * jnp.where(lane < 64, kw[p, q], kw[p, q + 1])
    turned = jnp.concatenate([a[:, 0:64] + a[:, 64:128] for a in acc], axis=1)

    for copy in passes.values():
        copy.wait_recv()
    for p, part in enumerate(rotate(1)):
        high, low = split(moved[p] + part)
        w[64 * p:64 * p + 64] = high
        w[128 + 64 * p:192 + 64 * p] = low
    cross(d2, w, s8)
    exchange = as_row(s8)
    c = lax.dot_general(ones, w[...], ROW_BY_ROW, preferred_element_type=F32)
    c = c[0:1] + c[1:2]
    coulomb = c[:, 0:128] + c[:, 128:256]

    pbuf[pair] = exchange + 2.0 * coulomb + turned
    p_copies = []
    for n, other in enumerate(pair_peers):
        copy = remote(pbuf.at[pair], pbuf.at[pair], p_send.at[n], p_recv.at[n], (row, other))
        copy.start()
        p_copies.append(copy)
    for copy in p_copies:
        copy.wait_recv()
    total = pbuf[0]
    for n in range(1, 8):
        total = total + pbuf[n]
    total = 2.0 * total
    out_ref[0:1, :] = total[:, 0:64]
    out_ref[1:2, :] = total[:, 64:128]

    for copies in (own.values(), cut.values(), passes.values(), f_copies.values(), p_copies, (over, f_over)):
        for copy in copies:
            copy.wait_send()

def per_device(slab_active, slab_general, kappa_general, kappa_window, density_one, density_two):
    dma, regular = pltpu.SemaphoreType.DMA, pltpu.SemaphoreType.REGULAR
    return pl.pallas_call(
        kernel,
        out_shape=jax.ShapeDtypeStruct((2, 64), F32),
        in_specs=[pl.BlockSpec(memory_space=pltpu.HBM)] * 6,
        out_specs=pl.BlockSpec(memory_space=pltpu.VMEM),
        scratch_shapes=[
            pltpu.VMEM((2, 64, 512), F32),
            pltpu.VMEM((2, 2, 32, 24, 512), F32),
            pltpu.VMEM((48, 64), F32),
            pltpu.SMEM((2, 64), F32),
            pltpu.VMEM((1, 512), F32),
            pltpu.VMEM((64, 64, 512), BF16),
            pltpu.VMEM((2, 2, 2, 2, 192, 512), BF16),
            pltpu.VMEM((2, 2, 2, 2, 192, 512), BF16),
            pltpu.VMEM((2, 2, 8, 24, 128), F32),
            pltpu.VMEM((128, 768), BF16),
            pltpu.VMEM((256, 512), BF16),
            pltpu.VMEM((64, 8, 256), F32),
            pltpu.VMEM((2, 64, 512), F32),
            pltpu.VMEM((2, 16, 1, 128), F32),
            pltpu.VMEM((8, 1, 128), F32),
            dma((9,)),
            regular((7,)),
            regular((8,)),
            regular((3, 7)),
            dma((7,)),
            dma((7,)),
            dma((4,)),
            dma((4,)),
            dma((2, 3)),
            dma((2, 3)),
            dma((2,)),
            dma((2,)),
            dma((15,)),
            dma((15,)),
            dma((7,)),
            dma((7,)),
        ],
        compiler_params=pltpu.CompilerParams(
            collective_id=0, has_side_effects=True, vmem_limit_bytes=48 * 2**20
        ),
        name="sigma",
    )(*(
        pltpu.with_memory_space_constraint(x, pltpu.HBM)
        for x in (
            slab_active,
            slab_general.reshape(2, 32, 48, 512),
            kappa_general,
            kappa_window,
            density_one.reshape(1, 512),
            density_two,
        )
    ))


def solution(mesh):
    in_specs = (
        P("rows", None, "pairs"),
        P("rows", None, "pairs"),
        P("rows", None),
        P("rows", None),
        P("pairs"),
        P(None, None, "pairs"),
    )
    out_specs = P("rows", None)
    return jax.shard_map(
        per_device, mesh=mesh, in_specs=in_specs, out_specs=out_specs, check_vma=False
    )
```

time: 32.4 us -> 26 us (0.80)
  local copies, waits for them, and re-layouts: 5.8 us -> 0.56 us
  Pallas kernels: 26.4 us -> 25.3 us
    unnamed x11 -> x1, local copies, waits for them, and re-layouts: 5.8 us -> 0.56 us
    pallas_call x1, Pallas kernels: 26.4 us -> 25.3 us  [per_device(): pl.pallas_call(kernel, out_shape=jax.ShapeDtypeStruct((2, 64), F32), in_s...]
where the time goes in v3:
time: 26 us; the launch traced here: 25.9 us
  Pallas kernels  25.3 us (97%)
  local copies, waits for them, and re-layouts  0.56 us (2%)
    pallas_call x1, Pallas kernels, per_device(): pl.pallas_call(kernel, out_shape=jax.ShapeDtypeStruct((2, 64), F32), in_s...  25.3 us
    unnamed x1, local copies, waits for them, and re-layouts  0.56 us

profile of v3, /device:TPU:1, one launch (start us, length us, event | category | flops | bytes accessed | tf_op | source)
XLA Modules:
  0.0 25.9 jit_solution(534778730068528198)
XLA Ops:
  0.0 25.3 %sigma.1 = f32[2,64]{1,0:T(2,128)S(1)} custom-call(f32[2,64,512]{2,1,0:T(8,128)} %sa_hbm.1, f32[2,32,48,512]{3,2,1,0:T(8,128)} %bitcast.2, f32[48,64]{1,0:T(8,128)} %kg_hbm.1, f32[2,64]{1,0:T(2,128)} %kw_hbm.1, f32[1,512]{1,0:T(1,128)} %bitcast.3, bf16[64,64,512]{2,1,0:T(8,128)(2,1)} %d2_hbm.1), custom_call_target="tpu_custom_call" | custom-call | tf_op jit(solution)/shard_map/sigma/pallas_call | solution.py:333
  25.3 0.6 %copy.8 = f32[2,64]{1,0:T(2,128)} copy(f32[2,64]{1,0:T(2,128)S(1)} %sigma.1) | data formatting | bytes 1024

commit v4 on v3

v4 whole, which is shorter than its diff:
```python
import jax
import jax.numpy as jnp
from jax import lax
from jax.experimental import pallas as pl
from jax.experimental.pallas import tpu as pltpu
from jax.sharding import PartitionSpec as P

MESH = pl.DeviceIdType.MESH
BF16, F32 = jnp.bfloat16, jnp.float32
ROW_BY_ROW = (((1,), (1,)), ((), ()))
PLAIN = (((1,), (0,)), ((), ()))

OWN = ((1, 3), (1, 2), (0, 3), (1, 1), (0, 2), (1, 0), (0, 1))
DIRECT = ((1, 1), (0, 1), (1, 3), (0, 3))


ORDER = (3, 1, 2, 0)


def own_slot(dy, dk):
    return dy * 4 + dk


def cut_slot(dy, dk):
    return ORDER.index(dk) * 2 + dy


def split(x):
    high = x.astype(BF16)
    return high, (x - high.astype(F32)).astype(BF16)


def cross(d2_ref, w_ref, s8_ref, groups=range(8)):
    sub = lax.broadcasted_iota(jnp.int32, (8, 256), 0)
    lane = lax.broadcasted_iota(jnp.int32, (8, 256), 1) % 64
    masks = [lane == sub + 8 * k for k in range(8)]
    group = 8
    for b in groups:
        r = lax.dot_general(
            d2_ref[b * group:(b + 1) * group].reshape(group * 64, 512), w_ref[...], ROW_BY_ROW,
            preferred_element_type=F32,
        )
        for t in range(group):
            acc = jnp.zeros((8, 256), F32)
            for k in range(8):
                at = (t * 8 + k) * 8
                acc = jnp.where(masks[k], r[at:at + 8, :], acc)
            s8_ref[b * group + t] = acc


def as_row(s8_ref):
    s = jnp.sum(s8_ref[...], axis=1).T
    pair = jnp.sum(s.reshape(2, 2, 64, 64), axis=(0, 2))
    return jnp.concatenate([pair[0:1], pair[1:2]], axis=1)


def kernel(
    sa_hbm, g_hbm, kg_hbm, kw_hbm, d1_hbm, d2_hbm, out_ref,
    sa, gbuf, kgin, kw, d1, d2, ghi, glo, cut_hi, cut_lo, kg, w, s8, moved, fall, pbuf,
    load_sem, near_here, far_here, pair_here, hop_here, own_send, own_recv, cut_send, cut_recv, pass_send, pass_recv,
    sib_send, sib_recv, f_send, f_recv, f_pass_send, f_pass_recv, p_send, p_recv,
):
    row, pair = lax.axis_index("rows"), lax.axis_index("pairs")
    core, chip = row % 2, row // 2
    ylo, z = chip // 8, chip % 8
    half, k = z // 4, z % 4
    x, yhi = pair // 2, pair % 2
    early, late = half == 0, half == 1

    def chip_of(cut, dy, dk):
        return (ylo ^ dy) * 8 + (half ^ cut) * 4 + (k ^ dk)

    def peer(cut, dy, dk):
        return (chip_of(cut, dy, dk) * 2 + core, pair)

    def signal(semaphore, device):
        pl.semaphore_signal(semaphore, inc=1, device_id=device, device_id_type=MESH)

    def remote(source, target, send, recv, device):
        return pltpu.make_async_remote_copy(
            source, target, send, recv, device_id=device, device_id_type=MESH
        )

    def is_later(dy, dk):
        return (k ^ dk) * 2 + (ylo ^ dy) > k * 2 + ylo

    sibling = (chip * 2 + 1 - core, pair)
    beside = [((chip ^ 1) * 2 + core, pair), ((chip ^ 1) * 2 + 1 - core, pair)]
    pair_peers = [pair ^ n for n in (5, 7, 4, 6, 3, 1, 2)]
    y = yhi * 2 + ylo

    def at(x, y, z):
        return (((y % 2) * 8 + z) * 2 + core, x * 2 + y // 2)

    hops = (
        (at((x + 1) % 4, y, z), x < 3),
        (at((x + 3) % 4, y, z), x > 0),
        (at(x, (y + 1) % 4, z), y < 3),
        (at(x, (y + 3) % 4, z), y > 0),
        (at(x, y, (z + 1) % 8), k < 3),
        (at(x, y, (z + 7) % 8), k > 0),
        (sibling, None),
    )

    def for_hops(condition, act):
        for n, (device, there) in enumerate(hops):
            @pl.when(condition if there is None else jnp.logical_and(condition, there))
            def _():
                act(n, device)

    kg_load = pltpu.make_async_copy(kg_hbm, kgin, load_sem.at[0])
    kg_load.start()

    barrier = pltpu.get_barrier_semaphore()

    def is_later_pair(other):
        return (other % 2) * 4 + other // 2 > yhi * 4 + x

    @pl.when(early)
    def _():
        for dy, dk in DIRECT:
            signal(barrier, peer(1, dy, dk))
        for dy, dk in OWN:
            @pl.when(is_later(dy, dk))
            def _():
                signal(barrier, peer(0, dy, dk))
        for other in pair_peers:
            @pl.when(is_later_pair(other))
            def _():
                signal(barrier, (row, other))
        signal(barrier, sibling)
        @pl.when(k % 2 == 0)
        def _():
            signal(barrier, beside[1])

    for_hops(late, lambda n, device: signal(barrier, device))

    sa_load = pltpu.make_async_copy(sa_hbm, sa, load_sem.at[1])
    sa_load.start()
    d2_load = pltpu.make_async_copy(d2_hbm, d2, load_sem.at[2])
    d2_load.start()
    d1_load = pltpu.make_async_copy(d1_hbm, d1, load_sem.at[3])
    d1_load.start()
    kw_load = pltpu.make_async_copy(kw_hbm, kw, load_sem.at[4])
    kw_load.start()
    g_loads = []
    for p in range(2):
        for h in range(2):
            load = pltpu.make_async_copy(
                g_hbm.at[p, :, pl.ds(h * 24, 24), :], gbuf.at[p, h], load_sem.at[5 + 2 * p + h]
            )
            g_loads.append(load)

    kg_load.wait()
    kg[0, core, 0] = jnp.concatenate([kgin[0:24, :], kgin[24:48, :]], axis=1)

    def inner(v):
        return jnp.where(jnp.logical_or(v == 0, v == 3), 0, 1)

    pl.semaphore_wait(
        barrier, jnp.where(early, 1 + 2 * k + ylo + 4 * yhi + x + k % 2, 8 + inner(x) + inner(y) + inner(k))
    )

    own = {}
    for n, (dy, dk) in enumerate(OWN):
        own[dy, dk] = remote(
            kg.at[0, core, 0], kg.at[0, core, own_slot(dy, dk)], own_send.at[n], own_recv.at[n], peer(0, dy, dk)
        )
    cut = {}
    for n, (dy, dk) in enumerate(DIRECT):
        cut[dy, dk] = remote(
            kg.at[0, core, 0], kg.at[1, core, cut_slot(dy, dk)], cut_send.at[n], cut_recv.at[n], peer(1, dy, dk)
        )

    @pl.when(late)
    def _():
        for copy in cut.values():
            copy.start()
        for n, (dy, dk) in enumerate(DIRECT):
            signal(far_here.at[n], peer(1, dy, dk))
        for_hops(late, lambda n, device: signal(hop_here.at[0, n ^ 1 if n < 6 else n], device))

    @pl.when(early)
    def _():
        for n, (dy, dk) in enumerate(OWN):
            @pl.when(jnp.logical_not(is_later(dy, dk)))
            def _():
                signal(near_here.at[n], peer(0, dy, dk))
                own[dy, dk].start()
        for n, other in enumerate(pair_peers):
            @pl.when(jnp.logical_not(is_later_pair(other)))
            def _():
                signal(pair_here.at[n], (row, other))
        @pl.when(k % 2 == 1)
        def _():
            signal(pair_here.at[7], beside[1])

    def next_round(step):
        for_hops(late, lambda n, device: pl.semaphore_wait(hop_here.at[step, n], 1))
        if step < 3:
            for_hops(late, lambda n, device: signal(hop_here.at[step + 1, n ^ 1 if n < 6 else n], device))

    sa_load.wait()
    high, low = split(sa[...].reshape(128, 512))
    w[0:128] = high
    w[128:256] = low
    d2_load.wait()
    for load in g_loads:
        load.start()
    cross(d2, w, s8, range(4))
    next_round(0)
    cross(d2, w, s8, range(4, 8))
    fall[0, core, 0] = as_row(s8)
    next_round(1)
    f_own = {}
    for n, (dy, dk) in enumerate(OWN):
        f_own[dy, dk] = remote(
            fall.at[0, core, 0], fall.at[0, core, own_slot(dy, dk)], f_send.at[n], f_recv.at[n], peer(0, dy, dk)
        )
    f_cut = {}
    for n, (dy, dk) in enumerate(DIRECT):
        f_cut[dy, dk] = remote(
            fall.at[0, core, 0], fall.at[1, core, cut_slot(dy, dk)], f_send.at[7 + n], f_recv.at[7 + n], peer(1, dy, dk)
        )

    @pl.when(late)
    def _():
        for copy in f_cut.values():
            copy.start()
        next_round(2)
        for dy, dk in OWN:
            own[dy, dk].start()
        for copy in f_own.values():
            copy.start()

    @pl.when(early)
    def _():
        for n, (dy, dk) in enumerate(OWN):
            @pl.when(is_later(dy, dk))
            def _():
                pl.semaphore_wait(near_here.at[n], 1)
                own[dy, dk].start()
        for copy in f_own.values():
            copy.start()

    for load in g_loads:
        load.wait()

    def split_general(n, _):
        p, h, c = n // 4, (n // 2) % 2, n % 2

        def put(high, low, chips):
            for s in range(0, len(chips), 2):
                a, b = split(jnp.concatenate([gbuf[p, h, chips[s + i] * 2 + c] for i in range(2)], axis=0))
                high[s * 24:s * 24 + 48, :] = a
                low[s * 24:s * 24 + 48, :] = b

        put(ghi.at[p, h, c], glo.at[p, h, c], [chip_of(0, s // 4, s % 4) for s in range(8)])
        for part in range(2):
            chips = [chip_of(1, s % 2, ORDER[s // 2]) for s in range(4 * part, 4 * part + 4)]
            put(cut_hi.at[part, p, h, c], cut_lo.at[part, p, h, c], chips)
        return 0

    lax.fori_loop(0, 8, split_general, 0)

    @pl.when(early)
    def _():
        for n, (dy, dk) in enumerate(DIRECT):
            pl.semaphore_wait(far_here.at[n], 1)
            cut[dy, dk].start()
        for copy in f_cut.values():
            copy.start()

    @pl.when(jnp.logical_and(early, k % 2 == 0))
    def _():
        pl.semaphore_wait(pair_here.at[7], 1)


    def handed_on(array, send, recv):
        copies = {}
        for n, dk in enumerate((3, 1)):
            mine = array.at[1, core, pl.ds(cut_slot(0, dk), 2)]
            theirs = array.at[1, core, pl.ds(cut_slot(0, dk ^ 1), 2)]
            for m, (target, device) in enumerate(((theirs, beside[0]), (theirs, beside[1]), (mine, sibling))):
                copies[n, m] = remote(mine, target, send.at[n, m], recv.at[n, m], device)
        return copies

    def hand_on(arriving, copies):
        for n, dk in enumerate((3, 1)):
            for dy in range(2):
                arriving[dy, dk].wait_recv()
            for m in range(3):
                copies[n, m].start()

    passes = handed_on(kg, pass_send, pass_recv)
    f_passes = handed_on(fall, f_pass_send, f_pass_recv)

    def rotate(blocks, high_of, low_of):
        rows = blocks.reshape(-1, 128)
        depth = 2 * rows.shape[0]
        x = rows.T
        high, low = split(jnp.concatenate([x[0:64], x[64:128]], axis=1))
        both = jnp.concatenate([high, low], axis=0)
        result = []
        for p in range(2):
            a = lax.dot_general(both, high_of(p).reshape(depth, 512), PLAIN, preferred_element_type=F32)
            b = lax.dot_general(high, low_of(p).reshape(depth, 512), PLAIN, preferred_element_type=F32)
            result.append(a[0:64] + a[64:128] + b)
        return result

    def rotate_cut(part):
        return rotate(kg[1, :, 4 * part:4 * part + 4], lambda p: cut_hi[part, p], lambda p: cut_lo[part, p])

    hand_on(cut, passes)
    for copy in own.values():
        copy.wait_recv()
    over = remote(kg.at[0, core], kg.at[0, core], sib_send.at[0], sib_recv.at[0], sibling)
    over.start()
    over.wait_recv()
    for p, part in enumerate(rotate(kg[0], lambda p: ghi[p], lambda p: glo[p])):
        moved[p] = part
    for n in range(2):
        passes[n, 2].wait_recv()
    for p, part in enumerate(rotate_cut(0)):
        moved[p] = moved[p] + part

    for copy in f_own.values():
        copy.wait_recv()
    f_over = remote(fall.at[0, core], fall.at[0, core], sib_send.at[1], sib_recv.at[1], sibling)
    f_over.start()
    hand_on(f_cut, f_passes)
    d1_load.wait()
    high, low = split(jnp.broadcast_to(d1[...], (16, 512)))
    line = lax.broadcasted_iota(jnp.int32, (16, 512), 0)
    ones = jnp.where(line == 0, high.astype(F32), jnp.where(line == 1, low.astype(F32), 0.0)).astype(BF16)
    for n in range(2):
        for m in range(2):
            passes[n, m].wait_recv()
    for p, part in enumerate(rotate_cut(1)):
        high, low = split(moved[p] + part)
        w[64 * p:64 * p + 64] = high
        w[128 + 64 * p:192 + 64 * p] = low
    cross(d2, w, s8)
    exchange = as_row(s8)
    c = lax.dot_general(ones, w[...], ROW_BY_ROW, preferred_element_type=F32)
    c = c[0:1] + c[1:2]
    coulomb = c[:, 0:128] + c[:, 128:256]

    kw_load.wait()
    f_over.wait_recv()
    for copy in f_passes.values():
        copy.wait_recv()
    lane = lax.broadcasted_iota(jnp.int32, (1, 128), 1)
    acc = [jnp.zeros((1, 128), F32) for _ in range(2)]
    for part in range(2):
        for slot in range(8):
            first = 4 * (chip_of(1, slot % 2, ORDER[slot // 2]) if part else chip_of(0, slot // 4, slot % 4))
            for c in range(2):
                f = fall[part, c, slot]
                q = first + 2 * c
                for p in range(2):
                    acc[p] = acc[p] + f * jnp.where(lane < 64, kw[p, q], kw[p, q + 1])
    turned = jnp.concatenate([a[:, 0:64] + a[:, 64:128] for a in acc], axis=1)

    next_round(3)
    pbuf[pair] = exchange + 2.0 * coulomb + turned
    p_copies = []
    for n, other in enumerate(pair_peers):
        @pl.when(jnp.logical_and(early, is_later_pair(other)))
        def _():
            pl.semaphore_wait(pair_here.at[n], 1)

        copy = remote(pbuf.at[pair], pbuf.at[pair], p_send.at[n], p_recv.at[n], (row, other))
        copy.start()
        p_copies.append(copy)
    for copies in (own.values(), cut.values(), passes.values(), f_own.values(), f_cut.values(), f_passes.values(), (over, f_over)):
        for copy in copies:
            copy.wait_send()
    for copy in p_copies:
        copy.wait_recv()
    total = pbuf[0]
    for n in range(1, 8):
        total = total + pbuf[n]
    total = 2.0 * total
    out_ref[0:1, :] = total[:, 0:64]
    out_ref[1:2, :] = total[:, 64:128]
    for copy in p_copies:
        copy.wait_send()


def per_device(slab_active, slab_general, kappa_general, kappa_window, density_one, density_two):
    dma, regular = pltpu.SemaphoreType.DMA, pltpu.SemaphoreType.REGULAR
    return pl.pallas_call(
        kernel,
        out_shape=jax.ShapeDtypeStruct((2, 64), F32),
        in_specs=[pl.BlockSpec(memory_space=pltpu.HBM)] * 6,
        out_specs=pl.BlockSpec(memory_space=pltpu.VMEM),
        scratch_shapes=[
            pltpu.VMEM((2, 64, 512), F32),
            pltpu.VMEM((2, 2, 32, 24, 512), F32),
            pltpu.VMEM((48, 64), F32),
            pltpu.SMEM((2, 64), F32),
            pltpu.VMEM((1, 512), F32),
            pltpu.VMEM((64, 64, 512), BF16),
            pltpu.VMEM((2, 2, 2, 192, 512), BF16),
            pltpu.VMEM((2, 2, 2, 192, 512), BF16),
            pltpu.VMEM((2, 2, 2, 2, 96, 512), BF16),
            pltpu.VMEM((2, 2, 2, 2, 96, 512), BF16),
            pltpu.VMEM((2, 2, 8, 24, 128), F32),
            pltpu.VMEM((256, 512), BF16),
            pltpu.VMEM((64, 8, 256), F32),
            pltpu.VMEM((2, 64, 512), F32),
            pltpu.VMEM((2, 2, 8, 1, 128), F32),
            pltpu.VMEM((8, 1, 128), F32),
            dma((9,)),
            regular((7,)),
            regular((4,)),
            regular((8,)),
            regular((4, 7)),
            dma((7,)),
            dma((7,)),
            dma((4,)),
            dma((4,)),
            dma((2, 3)),
            dma((2, 3)),
            dma((2,)),
            dma((2,)),
            dma((11,)),
            dma((11,)),
            dma((2, 3)),
            dma((2, 3)),
            dma((7,)),
            dma((7,)),
        ],
        compiler_params=pltpu.CompilerParams(
            collective_id=0, has_side_effects=True, vmem_limit_bytes=48 * 2**20
        ),
        name="sigma",
    )(*(
        pltpu.with_memory_space_constraint(x, pltpu.HBM)
        for x in (
            slab_active,
            slab_general.reshape(2, 32, 48, 512),
            kappa_general,
            kappa_window,
            density_one.reshape(1, 512),
            density_two,
        )
    ))


def solution(mesh):
    in_specs = (
        P("rows", None, "pairs"),
        P("rows", None, "pairs"),
        P("rows", None),
        P("rows", None),
        P("pairs"),
        P(None, None, "pairs"),
    )
    out_specs = P("rows", None)
    return jax.shard_map(
        per_device, mesh=mesh, in_specs=in_specs, out_specs=out_specs, check_vma=False
    )
```

time: 26 us -> 25.7 us (0.988)
  Pallas kernels: 25.3 us -> 25 us
    pallas_call x1, Pallas kernels: 25.3 us -> 25 us  [per_device(): pl.pallas_call(kernel, out_shape=jax.ShapeDtypeStruct((2, 64), F32), in_s...]
where the time goes in v4:
time: 25.7 us; the launch traced here: 25.6 us
  Pallas kernels  25 us (97%)
  local copies, waits for them, and re-layouts  0.56 us (2%)
    pallas_call x1, Pallas kernels, per_device(): pl.pallas_call(kernel, out_shape=jax.ShapeDtypeStruct((2, 64), F32), in_s...  25 us
    unnamed x1, local copies, waits for them, and re-layouts  0.56 us

profile of v4, /device:TPU:1, one launch (start us, length us, event | category | flops | bytes accessed | tf_op | source)
XLA Modules:
  0.0 25.6 jit_solution(8563512144381077986)
XLA Ops:
  0.0 25.0 %sigma.1 = f32[2,64]{1,0:T(2,128)S(1)} custom-call(f32[2,64,512]{2,1,0:T(8,128)} %sa_hbm.1, f32[2,32,48,512]{3,2,1,0:T(8,128)} %bitcast.2, f32[48,64]{1,0:T(8,128)} %kg_hbm.1, f32[2,64]{1,0:T(2,128)} %kw_hbm.1, f32[1,512]{1,0:T(1,128)} %bitcast.3, bf16[64,64,512]{2,1,0:T(8,128)(2,1)} %d2_hbm.1), custom_call_target="tpu_custom_call" | custom-call | tf_op jit(solution)/shard_map/sigma/pallas_call | solution.py:393
  25.0 0.6 %copy.8 = f32[2,64]{1,0:T(2,128)} copy(f32[2,64]{1,0:T(2,128)S(1)} %sigma.1) | data formatting | bytes 1024

commit v5 on v4

--- a/solution.py
+++ b/solution.py
@@ -319,16 +319,16 @@
     over.wait_recv()
     for p, part in enumerate(rotate(kg[0], lambda p: ghi[p], lambda p: glo[p])):
         moved[p] = part
-    for n in range(2):
-        passes[n, 2].wait_recv()
-    for p, part in enumerate(rotate_cut(0)):
-        moved[p] = moved[p] + part
 
     for copy in f_own.values():
         copy.wait_recv()
     f_over = remote(fall.at[0, core], fall.at[0, core], sib_send.at[1], sib_recv.at[1], sibling)
     f_over.start()
     hand_on(f_cut, f_passes)
+    for n in range(2):
+        passes[n, 2].wait_recv()
+    for p, part in enumerate(rotate_cut(0)):
+        moved[p] = moved[p] + part
     d1_load.wait()
     high, low = split(jnp.broadcast_to(d1[...], (16, 512)))
     line = lax.broadcasted_iota(jnp.int32, (16, 512), 0)

time: 25.7 us -> 25.7 us (level)
  no operation moved by 1% of the time
where the time goes in v5:
time: 25.7 us; the launch traced here: 25.6 us
  Pallas kernels  25 us (97%)
  local copies, waits for them, and re-layouts  0.56 us (2%)
    pallas_call x1, Pallas kernels, per_device(): pl.pallas_call(kernel, out_shape=jax.ShapeDtypeStruct((2, 64), F32), in_s...  25 us
    unnamed x1, local copies, waits for them, and re-layouts  0.56 us

profile of v5, /device:TPU:1, one launch (start us, length us, event | category | flops | bytes accessed | tf_op | source)
XLA Modules:
  0.0 25.6 jit_solution(2431313536060680197)
XLA Ops:
  0.0 25.0 %sigma.1 = f32[2,64]{1,0:T(2,128)S(1)} custom-call(f32[2,64,512]{2,1,0:T(8,128)} %sa_hbm.1, f32[2,32,48,512]{3,2,1,0:T(8,128)} %bitcast.2, f32[48,64]{1,0:T(8,128)} %kg_hbm.1, f32[2,64]{1,0:T(2,128)} %kw_hbm.1, f32[1,512]{1,0:T(1,128)} %bitcast.3, bf16[64,64,512]{2,1,0:T(8,128)(2,1)} %d2_hbm.1), custom_call_target="tpu_custom_call" | custom-call | tf_op jit(solution)/shard_map/sigma/pallas_call | solution.py:393
  25.0 0.6 %copy.8 = f32[2,64]{1,0:T(2,128)} copy(f32[2,64]{1,0:T(2,128)S(1)} %sigma.1) | data formatting | bytes 1024

commit v6 on v5

--- a/solution.py
+++ b/solution.py
@@ -329,6 +329,22 @@
         passes[n, 2].wait_recv()
     for p, part in enumerate(rotate_cut(0)):
         moved[p] = moved[p] + part
+    lane = lax.broadcasted_iota(jnp.int32, (1, 128), 1)
+
+    def turn(part, acc):
+        acc = list(acc)
+        for slot in range(8):
+            first = 4 * (chip_of(1, slot % 2, ORDER[slot // 2]) if part else chip_of(0, slot // 4, slot % 4))
+            for c in range(2):
+                f = fall[part, c, slot]
+                q = first + 2 * c
+                for p in range(2):
+                    acc[p] = acc[p] + f * jnp.where(lane < 64, kw[p, q], kw[p, q + 1])
+        return acc
+
+    kw_load.wait()
+    f_over.wait_recv()
+    acc = turn(0, [jnp.zeros((1, 128), F32) for _ in range(2)])
     d1_load.wait()
     high, low = split(jnp.broadcast_to(d1[...], (16, 512)))
     line = lax.broadcasted_iota(jnp.int32, (16, 512), 0)
@@ -346,20 +362,9 @@
     c = c[0:1] + c[1:2]
     coulomb = c[:, 0:128] + c[:, 128:256]
 
-    kw_load.wait()
-    f_over.wait_recv()
     for copy in f_passes.values():
         copy.wait_recv()
-    lane = lax.broadcasted_iota(jnp.int32, (1, 128), 1)
-    acc = [jnp.zeros((1, 128), F32) for _ in range(2)]
-    for part in range(2):
-        for slot in range(8):
-            first = 4 * (chip_of(1, slot % 2, ORDER[slot // 2]) if part else chip_of(0, slot // 4, slot % 4))
-            for c in range(2):
-                f = fall[part, c, slot]
-                q = first + 2 * c
-                for p in range(2):
-                    acc[p] = acc[p] + f * jnp.where(lane < 64, kw[p, q], kw[p, q + 1])
+    acc = turn(1, acc)
     turned = jnp.concatenate([a[:, 0:64] + a[:, 64:128] for a in acc], axis=1)
 
     next_round(3)

time: 25.7 us -> 25.6 us (level)
  no operation moved by 1% of the time
where the time goes in v6:
time: 25.6 us; the launch traced here: 25.5 us
  Pallas kernels  24.9 us (97%)
  local copies, waits for them, and re-layouts  0.56 us (2%)
    pallas_call x1, Pallas kernels, per_device(): pl.pallas_call(kernel, out_shape=jax.ShapeDtypeStruct((2, 64), F32), in_s...  24.9 us
    unnamed x1, local copies, waits for them, and re-layouts  0.56 us

profile of v6, /device:TPU:1, one launch (start us, length us, event | category | flops | bytes accessed | tf_op | source)
XLA Modules:
  0.0 25.5 jit_solution(18094586796247231484)
XLA Ops:
  0.0 24.9 %sigma.1 = f32[2,64]{1,0:T(2,128)S(1)} custom-call(f32[2,64,512]{2,1,0:T(8,128)} %sa_hbm.1, f32[2,32,48,512]{3,2,1,0:T(8,128)} %bitcast.2, f32[48,64]{1,0:T(8,128)} %kg_hbm.1, f32[2,64]{1,0:T(2,128)} %kw_hbm.1, f32[1,512]{1,0:T(1,128)} %bitcast.3, bf16[64,64,512]{2,1,0:T(8,128)(2,1)} %d2_hbm.1), custom_call_target="tpu_custom_call" | custom-call | tf_op jit(solution)/shard_map/sigma/pallas_call | solution.py:398
  24.9 0.6 %copy.8 = f32[2,64]{1,0:T(2,128)} copy(f32[2,64]{1,0:T(2,128)S(1)} %sigma.1) | data formatting | bytes 1024
